TPU v7x, 256 devices: a whole 4x4x8 slice. The times are simulated.
256 devices in a mesh: ep: 32 (over z, y), dp: 8 (over x, core).
Axes of the slice: x: 4, y: 4, z: 8, core: 2. Of those that a mesh axis runs over, the one named last changes fastest.
Arguments:
- tokens: bfloat16 [2048, 7168], P('ep', 'dp'), may hold values from -6 to 6
- gate_weight: bfloat16 [32, 7168, 2048], P('ep', None, 'dp'), may hold values from -0.0625 to 0.0625
- up_weight: bfloat16 [32, 7168, 2048], P('ep', None, 'dp'), may hold values from -0.0625 to 0.0625
- down_weight: bfloat16 [32, 2048, 7168], P('ep', None, 'dp'), may hold values from -0.125 to 0.125
- routes: int32 [2048, 8], P('ep'), may hold values from 0 to 31, all different within a row; in each aligned block of 64 rows (0 to 63, 64 to 127, ...) at most 20 rows name the same one
- route_weights: float32 [2048, 8], P('ep'), may hold values from 0.1 to 1
- slot_counts: int32 [2048], P('ep'), may hold values from 4 to 8
Outputs:
- mixed: bfloat16 [2048, 7168], P('ep', 'dp')
Inputs may be any that keep to these rules, and one draw needn't show every extreme that they name: `routes`: each row names 8 different experts; of the 64 rows of one index of ep at most 20 name one expert.
All inputs are finite; a program needn't handle non-finite values.
Results may differ from a plain program's by a relative error of at most 0.0057.
Values may be sent and summed in bfloat16 or wider, within the bound.
A program may use at most 128 MiB of HBM per device.

v0:
```python
import jax
import jax.numpy as jnp
from jax import lax
from jax.sharding import PartitionSpec as P


def targets(route_rows, count_rows, expert_count, capacity):
    row_count, pick_count = route_rows.shape
    active = lax.broadcasted_iota(jnp.int32, (row_count, pick_count), 1) < count_rows[:, None]
    flat_routes = route_rows.reshape(-1)
    live_mask = active.reshape(-1)
    one_hot = (
        (flat_routes[:, None] == lax.broadcasted_iota(jnp.int32, (1, expert_count), 1))
        & live_mask[:, None]
    ).astype(jnp.int32)
    before = jnp.cumsum(one_hot, axis=0) - one_hot
    position = jnp.sum(before * one_hot, axis=1)
    destination = jnp.where(live_mask, flat_routes * capacity + position, expert_count * capacity)
    return (destination.reshape(row_count, pick_count), active)


def shards(tokens, gate_weight, up_weight, down_weight, routes, route_weights, slot_counts):
    expert_count = lax.axis_size("ep")
    row_count, pick_count = routes.shape
    capacity = min(row_count, row_count * pick_count * 5 // (4 * expert_count))
    slot_total = expert_count * capacity
    destination, active = targets(routes, slot_counts, expert_count, capacity)
    chosen = jnp.any(
        destination[:, :, None] == lax.broadcasted_iota(jnp.int32, (1, 1, slot_total), 2), axis=1
    ).astype(jnp.bfloat16)
    gate_local = gate_weight[0]
    up_local = up_weight[0]
    down_local = down_weight[0]
    full_rows = lax.all_gather(tokens, "dp", axis=1, tiled=True)
    outgoing = jnp.einsum(
        "rs,rd->sd", chosen, full_rows, preferred_element_type=jnp.float32
    ).astype(jnp.bfloat16)
    arrived = lax.all_to_all(
        outgoing.reshape(expert_count, capacity, full_rows.shape[1]),
        "ep",
        split_axis=0,
        concat_axis=0,
        tiled=True,
    )
    arrived = arrived.reshape(slot_total, full_rows.shape[1])
    gate_act = jnp.dot(arrived, gate_local, preferred_element_type=jnp.float32)
    up_act = jnp.dot(arrived, up_local, preferred_element_type=jnp.float32)
    hidden = (jax.nn.silu(gate_act) * up_act).astype(jnp.bfloat16)
    projected = jnp.dot(
        lax.all_gather(hidden, "dp", axis=1, tiled=True),
        down_local,
        preferred_element_type=jnp.float32,
    )
    projected = projected.astype(jnp.bfloat16).reshape(expert_count, capacity, down_local.shape[1])
    returned = lax.all_to_all(projected, "ep", split_axis=0, concat_axis=0, tiled=True).reshape(
        slot_total, down_local.shape[1]
    )
    fetched = returned[jnp.minimum(destination, slot_total - 1)]
    weighting = jnp.where(active, route_weights, jnp.float32(0.0))
    mixed = jnp.sum(weighting[:, :, None] * fetched.astype(jnp.float32), axis=1)
    return mixed.astype(jnp.bfloat16)


def solution(mesh):
    placed = (
        P("ep", "dp"),
        P("ep", None, "dp"),
        P("ep", None, "dp"),
        P("ep", None, "dp"),
        P("ep", None),
        P("ep", None),
        P("ep"),
    )
    return jax.shard_map(
        shards, mesh=mesh, in_specs=placed, out_specs=P("ep", "dp"), check_vma=False
    )
```

profile of v0, /device:TPU:40, one launch (start us, length us, event | category | flops | bytes accessed | tf_op | source)
XLA Modules:
  0.0 414.9 jit_solution(16007096670415871167)
XLA Ops:
  6.5 0.0 all-gather.2.cloned.1.call-start
  6.5 0.8 copy.23
  7.3 0.1 eq.42
  7.4 0.1 eq.38
  7.5 0.7 lt.37
  8.2 0.7 iota_compare_fusion.3
  8.9 0.1 lt.38
  9.0 0.1 lt.39
  9.1 0.1 iota.33
  9.2 1.2 reduce-window.6
  10.4 0.2 slice_reduce_fusion
  10.6 0.1 copy.24
  10.7 0.1 lt.36
  10.8 0.1 fusion.19
  10.9 0.1 reduce_sum.21
  11.0 0.1 copy.27
  11.1 0.7 compare_select_fusion
  11.8 0.1 copy.28
  11.9 0.5 fusion.10
  12.4 14.2 %all_gather.6 = bf16[64,7168]{1,0:T(8,128)(2,1)S(1)} all-gather(bf16[64,896]{1,0:T(8,128)(2,1)} %param.7), channel_id=1, replica_groups=mesh['ep'=32,'dp'=8] {'dp'}, dimensions={1}, use_global_device_ids=true | all-gather | bytes 1032192 | tf_op jit(solution)/shard_map/all_gather | solution.py:34
  26.5 6.1 %convolution_convert_fusion = bf16[640,7168]{1,0:T(8,128)(2,1)} fusion(pred[64,640]{1,0:T(8,128)(4,1)S(1)} %fusion.10, bf16[64,7168]{1,0:T(8,128)(2,1)S(1)} %all_gather.6), kind=kOutput, calls=%fused_computation.1 | convolution fusion | flops 591790080 | bytes 10133504 | tf_op jit(solution)/shard_map/rs,rd->sd/dot_general | solution.py:35
  32.6 13.3 %reshape.77 = bf16[32,20,7168]{2,1,0:T(8,128)(2,1)} reshape(bf16[640,7168]{1,0:T(8,128)(2,1)} %convolution_convert_fusion) | data formatting | bytes 18350080 | tf_op jit(solution)/shard_map/reshape | solution.py:39
  45.9 252.5 %all_to_all.10 = bf16[32,20,7168]{2,1,0:T(8,128)(2,1)} all-to-all(bf16[32,20,7168]{2,1,0:T(8,128)(2,1)} %reshape.77), channel_id=1, replica_groups=mesh['ep'=32,'dp'=8] {'ep'}, dimensions={0} | all-to-all | bytes 18350080 | tf_op jit(solution)/shard_map/all_to_all | solution.py:38
  298.4 13.4 %reshape.78 = bf16[640,7168]{1,0:T(8,128)(2,1)} reshape(bf16[32,20,7168]{2,1,0:T(8,128)(2,1)} %all_to_all.10) | data formatting | bytes 18350080 | tf_op jit(solution)/shard_map/reshape | solution.py:45
  311.8 0.0 copy-start
  311.8 0.0 copy-start.3
  311.8 7.3 %fusion.4 = f32[640,256]{1,0:T(8,128)S(1)} fusion(bf16[640,7168]{1,0:T(8,128)(2,1)} %reshape.78, bf16[1,7168,256]{2,1,0:T(8,128)(2,1)} %param.8), kind=kOutput, calls=%fused_computation.6 | convolution fusion | flops 2348810240 | bytes 13500416 | tf_op jit(solution)/shard_map/dot_general | solution.py:46
  319.1 0.0 copy-done
  319.1 1.0 copy-done.3
  320.1 3.3 fusion.14
  323.3 0.0 all-gather.2.cloned.1.call-update
  323.4 29.4 %all-gather.2.cloned.1.call-done = bf16[640,2048]{1,0:T(8,128)(2,1)} async-done(((bf16[640,256]{1,0:T(8,128)(2,1)}), bf16[640,2048]{1,0:T(8,128)(2,1)}) %all-gather.2.cloned.1.call-update) | async-done | bytes 2621456 | tf_op jit(solution)/shard_map/all_gather | solution.py:50
  352.8 5.7 %fusion.7 = bf16[640,896]{1,0:T(8,128)(2,1)S(1)} fusion(bf16[640,2048]{1,0:T(8,128)(2,1)} %all-gather.2.cloned.1.call-done, bf16[1,2048,896]{2,1,0:T(8,128)(2,1)} %param.10), kind=kOutput, calls=%fused_computation.10 | convolution fusion | flops 2349383680 | bytes 7438336 | tf_op jit(solution)/shard_map/dot_general | solution.py:49
  358.5 0.0 copy-start.1
  358.5 0.0 copy-start.2
  358.5 1.2 reshape.79
  359.8 10.1 %all-to-all-start.1 = ((bf16[32,20,896]{2,1,0:T(8,128)(2,1)}), bf16[32,20,896]{2,1,0:T(8,128)(2,1)S(1)}, u32[]{:S(2)}, u32[]{:S(2)}) async-start(bf16[32,20,896]{2,1,0:T(8,128)(2,1)} %reshape.79), calls=%async_computation.1 | async-start | bytes 2752512 | tf_op jit(solution)/shard_map/all_to_all | solution.py:55
  369.8 0.1 copy.29
  369.9 0.1 reshape.83
  370.0 0.0 copy-done.1
  370.0 0.0 copy-done.2
  370.0 0.1 copy.22
  370.1 34.3 %all-to-all-done.1 = bf16[32,20,896]{2,1,0:T(8,128)(2,1)S(1)} async-done(((bf16[32,20,896]{2,1,0:T(8,128)(2,1)}), bf16[32,20,896]{2,1,0:T(8,128)(2,1)S(1)}, u32[]{:S(2)}, u32[]{:S(2)}) %all-to-all-start.1) | async-done | bytes 1146912 | tf_op jit(solution)/shard_map/all_to_all | solution.py:55
  404.5 0.3 reshape.80
  404.7 2.1 gather_fusion
  406.8 1.3 fusion.6
  (7 shorter events, 0.1 us)
Async XLA Ops:
  6.5 346.3 %all-gather.2.cloned.1.call-start = ((), (), s32[]{:S(2)}) async-start(), calls=%async_computation.2 | async-start | bytes 2949120 | tf_op jit(solution)/shard_map/all_gather | solution.py:50
  311.8 7.3 %copy-start = (bf16[640,7168]{1,0:T(8,128)(2,1)S(1)}, bf16[640,7168]{1,0:T(8,128)(2,1)}, u32[]{:S(2)}) copy-start(bf16[640,7168]{1,0:T(8,128)(2,1)} %reshape.78) | copy-start | bytes 27525124
  311.8 8.3 %copy-start.3 = (bf16[1,7168,256]{2,1,0:T(8,128)(2,1)S(1)}, bf16[1,7168,256]{2,1,0:T(8,128)(2,1)}, u32[]{:S(2)}) copy-start(bf16[1,7168,256]{2,1,0:T(8,128)(2,1)} %param.9) | copy-start | bytes 11010052
  358.5 11.5 %copy-start.1 = (s32[64]{0:T(128)S(1)}, s32[64]{0:T(128)}, u32[]{:S(2)}) copy-start(s32[64]{0:T(128)} %param.13) | copy-start | bytes 772
  358.5 11.5 %copy-start.2 = (f32[64,8]{0,1:T(8,128)S(1)}, f32[64,8]{0,1:T(8,128)}, u32[]{:S(2)}) copy-start(f32[64,8]{0,1:T(8,128)} %param.12) | copy-start | bytes 6148
  359.8 44.7 %all-to-all-start.1 = ((bf16[32,20,896]{2,1,0:T(8,128)(2,1)}), bf16[32,20,896]{2,1,0:T(8,128)(2,1)S(1)}, u32[]{:S(2)}, u32[]{:S(2)}) async-start(bf16[32,20,896]{2,1,0:T(8,128)(2,1)} %reshape.79), calls=%async_computation.1 | async-start | bytes 2752512 | tf_op jit(solution)/shard_map/all_to_all | solution.py:55
Sparse Core Ops, SparseCore 0:
  323.5 29.2 all-gather.1
where the time goes:
time: 417 us; the launch traced here: 415 us
  blocking collectives  267 us (64%)
  waiting for transfers between devices  63.8 us (15%)
  local copies, waits for them, and re-layouts  34 us (8%)
  matrix products  22.4 us (5%)
  between operations  13.5 us (3%)
  starting transfers between devices  10.1 us (2%)
  other arithmetic  4.42 us (1%)
    all_to_all x1, blocking collectives, shards(): lax.all_to_all(outgoing.reshape(expert_count, capacity, full_rows.shape[1...  253 us
    all_to_all x1, waiting for transfers between devices, shards(): lax.all_to_all(projected, 'ep', split_axis=0, concat_axis=0, tiled=True)  34.3 us
    all_gather x1, waiting for transfers between devices, shards(): lax.all_gather(hidden, 'dp', axis=1, tiled=True)  29.4 us
    all_gather x1, blocking collectives, shards(): full_rows = lax.all_gather(tokens, 'dp', axis=1, tiled=True)  14.2 us
    reshape x1, local copies, waits for them, and re-layouts, shards(): arrived = arrived.reshape(slot_total, full_rows.shape[1])  13.4 us
    reshape x1, local copies, waits for them, and re-layouts, shards(): outgoing.reshape(expert_count, capacity, full_rows.shape[1])  13.3 us
    all_to_all x1, starting transfers between devices, shards(): lax.all_to_all(projected, 'ep', split_axis=0, concat_axis=0, tiled=True)  10.1 us
  transfers between devices with their start and end apart: 2, of which 2 were waited for; matrix products, arithmetic and copies ran while one was open for 0% of the time, Pallas kernels for 0%

commit v1 on v0

v1 whole, which is shorter than its diff:
```python
import jax
import jax.numpy as jnp
from jax import lax
from jax.experimental import pallas as pl
from jax.experimental.pallas import tpu as pltpu
from jax.sharding import PartitionSpec as P

MESH = pl.DeviceIdType.MESH
NZ, NY, NX = 8, 4, 4
CAP = 20
Q = NZ * CAP
MARK = 1024.0
ORDER = (0, 1, 3, 2)
F32 = jnp.float32
BF16 = jnp.bfloat16


def kernel(
    tokens, routes, weights, counts, gate, up, down, mixed,
    rows, table, gate_w, up_w, down_w, place_t, choose, choose_t, picked, gath, hid, outs, back, part,
    carry, came, load_sem, send, recv,
):
    row_count, width = tokens.shape
    units = gate_w.shape[1]
    top = routes.shape[1]
    all_rows = NZ * row_count
    ep, dp = lax.axis_index("ep"), lax.axis_index("dp")
    z, y, x, core = ep // NY, ep % NY, dp // 2, dp % 2
    used = [0]

    def at_z(k):
        return (((z + k) % NZ) * NY + y, dp)

    def at_y(k):
        return (z * NY + (y + k) % NY, dp)

    def at_x(k):
        return (ep, ((x + k) % NX) * 2 + core)

    other = (ep, x * 2 + 1 - core)

    def link(src, dst, device):
        n = used[0]
        used[0] += 1
        return pltpu.make_async_remote_copy(
            src_ref=src, dst_ref=dst, send_sem=send.at[n], recv_sem=recv.at[n],
            device_id=device, device_id_type=MESH,
        )

    sent = []

    def go(copy):
        copy.start()
        sent.append(copy)
        return copy

    loads = [
        pltpu.make_async_copy(gate.at[0], gate_w, load_sem.at[0]),
        pltpu.make_async_copy(up.at[0], up_w, load_sem.at[1]),
        pltpu.make_async_copy(down.at[0], down_w, load_sem.at[2]),
    ]
    for load in loads:
        load.start()

    barrier = pltpu.get_barrier_semaphore()
    partners = [at_z(k) for k in range(1, NZ)] + [at_y(k) for k in range(1, NY)] + [at_x(1), at_x(-1), other]
    for device in partners:
        pl.semaphore_signal(barrier, inc=1, device_id=device, device_id_type=MESH)

    lane = lax.broadcasted_iota(jnp.int32, (row_count, 128), 1)
    dense = jnp.zeros((row_count, 128), F32)
    for k in range(top):
        live = jnp.logical_and(lane == routes[:, k : k + 1], counts[...] > k)
        dense = dense + jnp.where(live, weights[:, k : k + 1], 0.0)
    table[pl.ds(0, row_count), :] = dense

    pl.semaphore_wait(barrier, len(partners))

    def block(ref, k):
        return ref.at[pl.ds(k * row_count, row_count)]

    half = NZ // 2
    down_going = {1: go(link(tokens, block(rows, 1), at_z(-1)))}
    up_going = {NZ - 1: go(link(tokens, block(rows, NZ - 1), at_z(1)))}
    tables = [go(link(block(table, 0), block(table, NZ - k), at_z(k))) for k in range(1, NZ)]
    rows[pl.ds(0, row_count), :] = tokens[...]

    for copy in tables:
        copy.wait_recv()
    taken = jnp.where(table[...] > 0.0, 1.0, 0.0).astype(BF16)
    first = lax.broadcasted_iota(jnp.int32, (all_rows, all_rows), 0)
    second = lax.broadcasted_iota(jnp.int32, (all_rows, all_rows), 1)
    ahead = jnp.where(first < second, 1.0, jnp.where(first == second, MARK, 0.0)).astype(BF16)
    place_t[...] = lax.dot_general(taken, ahead, (((0,), (0,)), ((), ())), preferred_element_type=F32)
    behind = jnp.where(second < first, 1.0, jnp.where(first == second, MARK, 0.0)).astype(BF16)
    place = jnp.dot(behind, taken, preferred_element_type=F32)
    lanes = lax.broadcasted_iota(jnp.int32, (all_rows, 128), 1)
    scales = []
    for j in range(NY):
        expert = z * NY + (y + j) % NY
        slot = lax.broadcasted_iota(jnp.int32, (Q, all_rows), 0).astype(F32) + MARK
        choose[j] = jnp.where(place_t[pl.ds(expert, 1), :] == slot, 1.0, 0.0).astype(BF16)
        own = lanes == expert
        column = jnp.sum(jnp.where(own, place, 0.0), axis=1, keepdims=True)
        slot_t = lax.broadcasted_iota(jnp.int32, (all_rows, Q), 1).astype(F32) + MARK
        choose_t[j] = jnp.where(column == slot_t, 1.0, 0.0).astype(BF16)

    for k in range(1, half + 1):
        down_going[k].wait_recv()
        if k < half:
            down_going[k + 1] = go(link(block(rows, k), block(rows, k + 1), at_z(-1)))
            m = NZ - k
            up_going[m].wait_recv()
            if m - 1 > half:
                up_going[m - 1] = go(link(block(rows, m), block(rows, m - 1), at_z(1)))

    to_expert = {}

    def pick(j):
        chosen = jnp.dot(choose[j], rows[...], preferred_element_type=F32).astype(BF16)
        if j == 0:
            gath[0, 0, 0] = chosen
        else:
            picked[j - 1] = chosen
            r = NY - j
            to_expert[r] = go(link(picked.at[j - 1], gath.at[r, 0, 0], at_y(j)))

    rings = {}

    def ring_a(buf, name, r):
        mine = buf.at[r, 0, 0]
        rings[name, r] = [
            go(link(mine, buf.at[r, 3, 0], at_x(1))),
            go(link(mine, buf.at[r, 1, 0], at_x(-1))),
            go(link(mine, buf.at[r, 0, 1], other)),
        ]

    def ring_b(buf, name, r):
        ring = rings[name, r]
        low, high = pl.ds(0, Q // 2), pl.ds(Q // 2, Q // 2)
        ring[0].wait_recv()
        ring.append(go(link(buf.at[r, 3, 0, low], buf.at[r, 2, 0, low], at_x(1))))
        ring.append(go(link(buf.at[r, 3, 0], buf.at[r, 3, 1], other)))
        ring[1].wait_recv()
        ring.append(go(link(buf.at[r, 1, 0, high], buf.at[r, 2, 0, high], at_x(-1))))
        ring.append(go(link(buf.at[r, 1, 0], buf.at[r, 1, 1], other)))

    def ring_c(buf, name, r):
        ring = rings[name, r]
        ring[3].wait_recv()
        ring[5].wait_recv()
        ring.append(go(link(buf.at[r, 2, 0], buf.at[r, 2, 1], other)))

    STEPS = ((0, 0, None), (3, 0, None), (1, 0, None), (0, 1, 2), (3, 1, 4), (1, 1, 6), (2, 0, None), (2, 1, 7))

    def slice_at(dx, dc):
        return ((x + dx) % NX) * 2 + (core if dc == 0 else 1 - core)

    def stage_a(r):
        if r != 0:
            to_expert[r].wait_recv()
        ring_a(gath, "g", r)

    def stage_b(r):
        ring_b(gath, "g", r)

    def stage_c(r):
        ring_c(gath, "g", r)
        gate_acc = jnp.zeros((Q, units), F32)
        up_acc = jnp.zeros((Q, units), F32)
        for dx, dc, awaited in STEPS:
            if awaited is not None:
                rings["g", r][awaited].wait_recv()
            at = pl.ds(pl.multiple_of(slice_at(dx, dc) * width, width), width)
            piece = gath[r, dx, dc]
            gate_acc = gate_acc + jnp.dot(piece, gate_w[at, :], preferred_element_type=F32)
            up_acc = up_acc + jnp.dot(piece, up_w[at, :], preferred_element_type=F32)
        hid[r, 0, 0] = (gate_acc / (1.0 + jnp.exp(-gate_acc)) * up_acc).astype(BF16)
        ring_a(hid, "h", r)

    def stage_d(r):
        ring_b(hid, "h", r)

    from_expert = {}

    def stage_e(r):
        ring_c(hid, "h", r)
        acc = jnp.zeros((Q, width), F32)
        for dx, dc, awaited in STEPS:
            if awaited is not None:
                rings["h", r][awaited].wait_recv()
            at = pl.ds(pl.multiple_of(slice_at(dx, dc) * units, units), units)
            acc = acc + jnp.dot(hid[r, dx, dc], down_w[at, :], preferred_element_type=F32)
        if r == 0:
            back[0] = acc.astype(BF16)
        else:
            outs[r - 1] = acc.astype(BF16)
            from_expert[NY - r] = go(link(outs.at[r - 1], back.at[NY - r], at_y(r)))

    a, b, c, d = ORDER
    pick(0)
    stage_a(0)
    for j in (1, 3, 2):
        pick(j)
    loads[0].wait()
    loads[1].wait()
    loads[2].wait()
    stage_a(b)
    stage_b(a)
    stage_a(c)
    stage_b(b)
    stage_c(a)
    stage_a(d)
    stage_b(c)
    stage_c(b)
    stage_d(a)
    stage_b(d)
    stage_c(c)
    stage_d(b)
    stage_e(a)
    stage_c(d)
    stage_d(c)
    stage_e(b)
    stage_d(d)
    stage_e(c)
    stage_e(d)

    for j in range(1, NY):
        from_expert[j].wait_recv()

    def weighted(k):
        span = pl.ds(k * row_count, row_count)
        total = jnp.zeros((row_count, width), F32)
        lanes_k = lax.broadcasted_iota(jnp.int32, (row_count, 128), 1)
        for j in range(NY):
            expert = z * NY + (y + j) % NY
            scale = jnp.sum(jnp.where(lanes_k == expert, table[span, :], 0.0), axis=1, keepdims=True)
            fetched = jnp.dot(choose_t[j, span, :], back[j], preferred_element_type=F32)
            total = total + scale * fetched
        return total

    part[half] = weighted(half).astype(BF16)
    up_sum = go(link(part.at[half], came.at[half - 1], at_z(1)))
    part[half + 1] = weighted(half + 1).astype(BF16)
    down_sum = go(link(part.at[half + 1], came.at[half + 1], at_z(-1)))
    for k in range(half - 1, 0, -1):
        mine = weighted(k)
        up_sum.wait_recv()
        part[k] = (mine + came[k].astype(F32)).astype(BF16)
        up_sum = go(link(part.at[k], came.at[k - 1], at_z(1)))
        m = NZ - k
        if m > half + 1:
            mine = weighted(m)
            down_sum.wait_recv()
            part[m] = (mine + came[m - 1].astype(F32)).astype(BF16)
            down_sum = go(link(part.at[m], came.at[m], at_z(-1)))
    mine = weighted(0)
    up_sum.wait_recv()
    down_sum.wait_recv()
    mixed[...] = (mine + came[0].astype(F32) + came[NZ - 1].astype(F32)).astype(BF16)
    for copy in sent:
        copy.wait_send()


COPIES = 96


def shards(tokens, gate_weight, up_weight, down_weight, routes, route_weights, slot_counts):
    row_count, width = tokens.shape
    _, depth, units = gate_weight.shape
    hidden = down_weight.shape[1]
    vmem = pl.BlockSpec(memory_space=pltpu.VMEM)
    hbm = pl.BlockSpec(memory_space=pl.ANY)
    all_rows = NZ * row_count
    return pl.pallas_call(
        kernel,
        out_shape=jax.ShapeDtypeStruct((row_count, width), BF16),
        in_specs=[vmem] * 4 + [hbm] * 3,
        out_specs=vmem,
        scratch_shapes=[
            pltpu.VMEM((all_rows, width), BF16),
            pltpu.VMEM((all_rows, 128), F32),
            pltpu.VMEM((depth, units), BF16),
            pltpu.VMEM((depth, units), BF16),
            pltpu.VMEM((hidden, width), BF16),
            pltpu.VMEM((128, all_rows), F32),
            pltpu.VMEM((NY, Q, all_rows), BF16),
            pltpu.VMEM((NY, all_rows, Q), BF16),
            pltpu.VMEM((NY - 1, Q, width), BF16),
            pltpu.VMEM((NY, NX, 2, Q, width), BF16),
            pltpu.VMEM((NY, NX, 2, Q, units), BF16),
            pltpu.VMEM((NY - 1, Q, width), BF16),
            pltpu.VMEM((NY, Q, width), BF16),
            pltpu.VMEM((NZ, row_count, width), BF16),
            pltpu.VMEM((8, 128), F32),
            pltpu.VMEM((NZ, row_count, width), BF16),
            pltpu.SemaphoreType.DMA((3,)),
            pltpu.SemaphoreType.DMA((COPIES,)),
            pltpu.SemaphoreType.DMA((COPIES,)),
        ],
        compiler_params=pltpu.CompilerParams(
            collective_id=0, has_side_effects=True, vmem_limit_bytes=60 * 1024 * 1024
        ),
    )(tokens, routes, route_weights, slot_counts[:, None], gate_weight, up_weight, down_weight)


def solution(mesh):
    placed = (
        P("ep", "dp"),
        P("ep", None, "dp"),
        P("ep", None, "dp"),
        P("ep", None, "dp"),
        P("ep", None),
        P("ep", None),
        P("ep"),
    )
    return jax.shard_map(
        shards, mesh=mesh, in_specs=placed, out_specs=P("ep", "dp"), check_vma=False
    )
```

time: 417 us -> 125 us (0.30)
  blocking collectives: 267 us -> 0 us
  Pallas kernels: 0 us -> 119 us
  waiting for transfers between devices: 63.8 us -> 0 us
  local copies, waits for them, and re-layouts: 34 us -> 5.66 us
  matrix products: 22.4 us -> 0 us
  between operations: 13.5 us -> 0.01 us
  starting transfers between devices: 10.1 us -> 0 us
  other arithmetic: 4.42 us -> 0 us
    all_to_all x1 -> x0, blocking collectives: 253 us -> none  [shards(): lax.all_to_all(outgoing.reshape(expert_count, capacity, full_rows.shape[1...]
    pallas_call x0 -> x1, Pallas kernels: none -> 119 us  [shards(): pl.pallas_call(kernel, out_shape=jax.ShapeDtypeStruct((row_count, width),...]
    all_to_all x1 -> x0, waiting for transfers between devices: 34.3 us -> none  [shards(): lax.all_to_all(projected, 'ep', split_axis=0, concat_axis=0, tiled=True)]
    all_gather x1 -> x0, waiting for transfers between devices: 29.4 us -> none  [shards(): lax.all_gather(hidden, 'dp', axis=1, tiled=True)]
    reshape x4 -> x0, local copies, waits for them, and re-layouts: 28.1 us -> none  [the longest x1 13.4 us: shards(): arrived = arrived.reshape(slot_total, full_rows.shape[1])]
    dot_general x4 -> x0, matrix products: 22.4 us -> none  [the longest x1 7.32 us: shards(): gate_act = jnp.dot(arrived, gate_local, preferred_element_type=jnp.float32)]
    all_gather x1 -> x0, blocking collectives: 14.2 us -> none  [shards(): full_rows = lax.all_gather(tokens, 'dp', axis=1, tiled=True)]
    all_to_all x1 -> x0, starting transfers between devices: 10.1 us -> none  [shards(): lax.all_to_all(projected, 'ep', split_axis=0, concat_axis=0, tiled=True)]
  transfers between devices with their start and end apart: 2 -> 0, of which waited for: 2 -> 0; matrix products, arithmetic and copies ran while one was open for 0% -> 0% of each run, Pallas kernels for 0% -> 0%
where the time goes in v1:
time: 125 us
  Pallas kernels  119 us (95%)
  local copies, waits for them, and re-layouts  5.66 us (5%)
    pallas_call x1, Pallas kernels, shards(): pl.pallas_call(kernel, out_shape=jax.ShapeDtypeStruct((row_count, width),...  119 us
    unnamed x3, local copies, waits for them, and re-layouts  4.32 us

profile of v1, /device:TPU:40, one launch (start us, length us, event | category | flops | bytes accessed | tf_op | source)
XLA Modules:
  0.0 124.5 jit_solution(17063227056539953466)
XLA Ops:
  0.0 1.4 %copy.8.routes = s32[64,8]{1,0:T(8,128)} copy(s32[64,8]{0,1:T(8,128)} %param.11) | data formatting | bytes 4096 | tf_op args[4]
  1.4 1.4 %copy.9.weights = f32[64,8]{1,0:T(8,128)} copy(f32[64,8]{0,1:T(8,128)} %param.12) | data formatting | bytes 4096 | tf_op args[5]
  2.8 1.3 %copy.10.counts = s32[64,1]{1,0:T(8,128)} copy(s32[64,1]{0,1:T(1,128)} %bitcast.1) | data formatting | bytes 512 | tf_op jit(solution)/shard_map/broadcast_in_dim | solution.py:304
  4.1 118.9 %shard_map.73 = bf16[64,896]{1,0:T(8,128)(2,1)} custom-call(bf16[64,896]{1,0:T(8,128)(2,1)} %tokens.1, s32[64,8]{1,0:T(8,128)} %copy.8.routes, f32[64,8]{1,0:T(8,128)} %copy.9.weights, s32[64,1]{1,0:T(8,128)} %copy.10.counts, bf16[1,7168,256]{2,1,0:T(8,128)(2,1)} %gate.1, bf16[1,7168,256]{2,1,0:T(8,128)(2,1)} %up.1, bf16[1,2048,896]{2,1,0:T(8,128)(2,1)} %down.1), custom_call_target="tpu_custom_call" | custom-call | tf_op jit(solution)/shard_map/pallas_call | solution.py:275
  123.0 1.6 %copy.12 = bf16[64,896]{1,0:T(8,128)(2,1)} copy(bf16[64,896]{1,0:T(8,128)(2,1)} %shard_map.73) | data formatting | bytes 229376

commit v2 on v0

v2 whole, which is shorter than its diff:
```python
import jax
import jax.numpy as jnp
from jax import lax
from jax.experimental import pallas as pl
from jax.experimental.pallas import tpu as pltpu
from jax.sharding import PartitionSpec as P

MESH = pl.DeviceIdType.MESH
NZ, NY, NX = 8, 4, 4
CAP = 20
EXPERTS = 32
TAG = 128
GROUPS = ((0, 1, 7, 2), (6, 3, 5, 4))
BLOCKS = GROUPS[0] + GROUPS[1]
G = len(GROUPS)
PER = len(GROUPS[0])
Q = PER * CAP
SIDE = (0, 1, 3, 2)
MARK = 1024.0
DIRECT = ((0, 3), (0, 2))
F32 = jnp.float32
BF16 = jnp.bfloat16
SCHEDULE = (
    "z1", "z2", "p0", "a0", "p1", "p3", "p2", "z3", "b0", "a1", "z4", "p4", "a4", "p5", "p7", "p6", "c0",
    "b1", "a5", "m0", "c1", "b4", "a6", "e0", "m1", "c4", "b5", "a7", "f0", "e1", "m4", "c5", "b6", "a3",
    "f1", "e4", "m5", "c6", "b7", "a2", "f4", "e5", "m6", "c7", "b3", "f5", "e6", "m7", "c3", "b2", "f6",
    "e7", "m3", "f7", "c2", "e3", "m2", "f3", "s1", "e2", "f2", "s0", "s2",
)


def kernel(
    tokens, routes, weights, counts, gate, up, down, mixed,
    rows, gate_w, up_w, down_w, place_t, choose, choose_t, picked, gath, hid, outs, back, part, came,
    load_sem, send, recv,
):
    row_count, width = tokens.shape
    units = gate_w.shape[1]
    top = routes.shape[0]
    span = PER * row_count
    ep, dp = lax.axis_index("ep"), lax.axis_index("dp")
    z, y, x, core = ep // NY, ep % NY, dp // 2, dp % 2
    used = [0]
    sent = []

    def at_z(k):
        return (((z + k) % NZ) * NY + y, dp)

    def at_y(k):
        return (z * NY + (y + k) % NY, dp)

    def at_x(k):
        return (ep, ((x + k) % NX) * 2 + core)

    other = (ep, x * 2 + 1 - core)

    def go(src, dst, device):
        n = used[0]
        used[0] += 1
        copy = pltpu.make_async_remote_copy(
            src_ref=src, dst_ref=dst, send_sem=send.at[n], recv_sem=recv.at[n],
            device_id=device, device_id_type=MESH,
        )
        copy.start()
        sent.append(copy)
        return copy

    loads = [
        pltpu.make_async_copy(gate.at[0], gate_w, load_sem.at[0]),
        pltpu.make_async_copy(up.at[0], up_w, load_sem.at[1]),
        pltpu.make_async_copy(down.at[0], down_w, load_sem.at[2]),
    ]
    for load in loads:
        load.start()

    barrier = pltpu.get_barrier_semaphore()
    partners = [at_z(1), at_z(-1), at_z(2), at_z(-2), at_z(3), at_z(-3), at_x(2), at_y(1), at_y(2), at_y(3), at_x(1), at_x(-1), other]
    for device in partners:
        pl.semaphore_signal(barrier, inc=1, device_id=device, device_id_type=MESH)

    expert_at = lax.broadcasted_iota(jnp.int32, (TAG, row_count), 0) % EXPERTS
    dense = jnp.zeros((TAG, row_count), F32)
    for k in range(top):
        live = jnp.logical_and(expert_at == routes[k : k + 1, :], counts[...] > k)
        dense = dense + jnp.where(live, weights[k : k + 1, :], 0.0)
    dense = jnp.concatenate([dense, jnp.zeros((TAG, TAG - row_count), F32)], axis=1).T[:row_count]
    high = dense.astype(BF16).astype(F32)
    middle = (dense - high).astype(BF16).astype(F32)
    low = dense - high - middle
    term = lax.broadcasted_iota(jnp.int32, (row_count, TAG), 1) // EXPERTS
    tag = jnp.where(term == 0, high, jnp.where(term == 1, middle, jnp.where(term == 2, low, 0.0)))
    rows[pl.ds(0, row_count), pl.ds(width, TAG)] = tag.astype(BF16)
    rows[pl.ds(0, row_count), pl.ds(0, width)] = tokens[...]

    pl.semaphore_wait(barrier, len(partners))

    half_rows = row_count // 2

    def block(k, h):
        return rows.at[pl.ds(BLOCKS.index(k) * row_count + h * half_rows, half_rows)]

    moves = {}

    def onward(k, h, step):
        moves[(k + step) % NZ, h] = go(block(k, h), block((k + step) % NZ, h), at_z(-step))

    for h in (0, 1):
        onward(0, h, 1)
        onward(0, 1 - h, -1)

    def hop(k):
        for h in (0, 1):
            if k < NZ // 2:
                moves[k, h].wait_recv()
                if k < NZ // 2 - 1 or h == 0:
                    onward(k, h, 1)
                moves[NZ - k, 1 - h].wait_recv()
                if k < NZ // 2 - 1 or h == 0:
                    onward(NZ - k, 1 - h, -1)
            else:
                moves[k, h].wait_recv()

    def group_tags(g):
        return rows[pl.ds(g * span, span), pl.ds(width, TAG)]

    def places(g):
        taken = jnp.where(group_tags(g).astype(F32) > 0.0, 1.0, 0.0).astype(BF16)
        first = lax.broadcasted_iota(jnp.int32, (span, span), 0)
        second = lax.broadcasted_iota(jnp.int32, (span, span), 1)
        ahead = jnp.where(first < second, 1.0, jnp.where(first == second, MARK, 0.0)).astype(BF16)
        place_t[...] = lax.dot_general(taken, ahead, (((0,), (0,)), ((), ())), preferred_element_type=F32)
        behind = jnp.where(second < first, 1.0, jnp.where(first == second, MARK, 0.0)).astype(BF16)
        place = jnp.dot(behind, taken, preferred_element_type=F32)
        lanes = lax.broadcasted_iota(jnp.int32, (span, TAG), 1)
        slot = lax.broadcasted_iota(jnp.int32, (Q, span), 0).astype(F32) + MARK
        slot_t = lax.broadcasted_iota(jnp.int32, (span, Q), 1).astype(F32) + MARK
        for j in range(NY):
            expert = z * NY + (y + j) % NY
            choose[g, j] = jnp.where(place_t[pl.ds(expert, 1), :] == slot, 1.0, 0.0).astype(BF16)
            column = jnp.sum(jnp.where(lanes == expert, place, 0.0), axis=1, keepdims=True)
            choose_t[g, j] = jnp.where(column == slot_t, 1.0, 0.0).astype(BF16)

    def spot(q):
        return pl.ds(q * Q, Q)

    to_expert = {}

    def pick(g, j):
        if j == 0:
            places(g)
        source = rows[pl.ds(g * span, span), pl.ds(0, width)]
        chosen = jnp.dot(choose[g, j], source, preferred_element_type=F32).astype(BF16)
        q = SIDE.index((NY - j) % NY)
        if j == 0:
            gath[g, 0, 0, spot(q), :] = chosen
        else:
            picked[g, j - 1] = chosen
            to_expert[g, q] = go(picked.at[g, j - 1], gath.at[g, 0, 0, spot(q)], at_y(j))

    ring = {}

    def x_start(g, q):
        if (g, q) in to_expert:
            to_expert[g, q].wait_recv()
        at = spot(q)
        mine = gath.at[g, 0, 0, at]
        ring[g, q, 3, 0] = go(mine, gath.at[g, 3, 0, at], at_x(1))
        ring[g, q, 1, 0] = go(mine, gath.at[g, 1, 0, at], at_x(-1))
        ring[g, q, 0, 1] = go(mine, gath.at[g, 0, 1, at], other)

    def share(g, q, dx):
        at = spot(q)
        ring[g, q, dx, 1] = go(gath.at[g, dx, 0, at], gath.at[g, dx, 1, at], other)

    def x_forward(g, q):
        at = spot(q)
        ring[g, q, 3, 0].wait_recv()
        if q % 2 == 0:
            ring[g, q, 2, 0] = go(gath.at[g, 3, 0, at], gath.at[g, 2, 0, at], at_x(1))
        share(g, q, 3)
        ring[g, q, 1, 0].wait_recv()
        if q % 2 == 1:
            ring[g, q, 2, 0] = go(gath.at[g, 1, 0, at], gath.at[g, 2, 0, at], at_x(-1))
        share(g, q, 1)

    def x_last(g, q):
        ring[g, q, 2, 0].wait_recv()
        share(g, q, 2)

    STEPS = ((0, 0), (3, 0), (1, 0), (2, 0), (0, 1), (3, 1), (1, 1), (2, 1))
    waited = []

    def slice_at(dx, dc):
        return ((x + dx) % NX) * 2 + (core if dc == 0 else 1 - core)

    hops = {}

    def first_half(g, q):
        if not waited:
            waited.append(1)
            for load in loads:
                load.wait()
        at = spot(q)
        gate_acc = jnp.zeros((Q, units), F32)
        up_acc = jnp.zeros((Q, units), F32)
        for dx, dc in STEPS:
            if dc == 1:
                ring[g, q, dx, 1].wait_recv()
            deep = pl.ds(pl.multiple_of(slice_at(dx, dc) * width, width), width)
            piece = gath[g, dx, dc, at, :]
            gate_acc = gate_acc + jnp.dot(piece, gate_w[deep, :], preferred_element_type=F32)
            up_acc = up_acc + jnp.dot(piece, up_w[deep, :], preferred_element_type=F32)
        hid[g, 0, 0, at, :] = (gate_acc / (1.0 + jnp.exp(-gate_acc)) * up_acc).astype(BF16)
        mine = hid.at[g, 0, 0, at]
        hops[g, q, 3, 0] = go(mine, hid.at[g, 3, 0, at], at_x(1))
        hops[g, q, 1, 0] = go(mine, hid.at[g, 1, 0, at], at_x(-1))
        if (g, q) in DIRECT:
            hops[g, q, 2, 0] = go(mine, hid.at[g, 2, 0, at], at_x(2))
        hops[g, q, 0, 1] = go(mine, hid.at[g, 0, 1, at], other)

    def hidden_forward(g, q):
        at = spot(q)
        for dx, step in ((3, 1), (1, -1)):
            hops[g, q, dx, 0].wait_recv()
            if (g, q) not in DIRECT and q % 2 == (dx == 1):
                hops[g, q, 2, 0] = go(hid.at[g, dx, 0, at], hid.at[g, 2, 0, at], at_x(step))
            hops[g, q, dx, 1] = go(hid.at[g, dx, 0, at], hid.at[g, dx, 1, at], other)

    from_expert = {}

    def second_half(g, q):
        at = spot(q)
        hops[g, q, 2, 0].wait_recv()
        hops[g, q, 2, 1] = go(hid.at[g, 2, 0, at], hid.at[g, 2, 1, at], other)
        acc = jnp.zeros((Q, width), F32)
        for dx, dc in STEPS:
            if dc == 1:
                hops[g, q, dx, 1].wait_recv()
            deep = pl.ds(pl.multiple_of(slice_at(dx, dc) * units, units), units)
            acc = acc + jnp.dot(hid[g, dx, dc, at, :], down_w[deep, :], preferred_element_type=F32)
        r = SIDE[q]
        if r == 0:
            back[g, 0] = acc.astype(BF16)
        else:
            outs[g, r - 1] = acc.astype(BF16)
            from_expert[g, NY - r] = go(outs.at[g, r - 1], back.at[g, NY - r], at_y(r))

    def weighted(k):
        n = BLOCKS.index(k)
        g, at = n // PER, pl.ds(n % PER * row_count, row_count)
        tags = rows[pl.ds(n * row_count, row_count), pl.ds(width, TAG)].astype(F32)
        lanes = lax.broadcasted_iota(jnp.int32, (row_count, TAG), 1) % EXPERTS
        total = jnp.zeros((row_count, width), F32)
        for j in range(NY):
            expert = z * NY + (y + j) % NY
            scale = jnp.sum(jnp.where(lanes == expert, tags, 0.0), axis=1, keepdims=True)
            fetched = jnp.dot(choose_t[g, j, at, :], back[g, j], preferred_element_type=F32)
            total = total + scale * fetched
        return total

    def returned(g):
        for j in range(1, NY):
            from_expert[g, j].wait_recv()

    sums = {}

    def far_sums():
        returned(1)
        part[4] = weighted(4).astype(BF16)
        sums[3] = go(part.at[4], came.at[0], at_z(1))
        part[5] = weighted(5).astype(BF16)
        sums[6] = go(part.at[5], came.at[1], at_z(-1))
        mine = weighted(3)
        sums[3].wait_recv()
        part[3] = (mine + came[0].astype(F32)).astype(BF16)
        sums[0, 3] = go(part.at[3], came.at[2], at_z(3))
        mine = weighted(6)
        sums[6].wait_recv()
        part[6] = (mine + came[1].astype(F32)).astype(BF16)
        sums[0, 6] = go(part.at[6], came.at[3], at_z(-2))

    def near_sums():
        returned(0)
        part[2] = weighted(2).astype(BF16)
        sums[0, 2] = go(part.at[2], came.at[4], at_z(2))
        part[1] = weighted(1).astype(BF16)
        sums[0, 1] = go(part.at[1], came.at[5], at_z(1))
        part[7] = weighted(7).astype(BF16)
        sums[0, 7] = go(part.at[7], came.at[6], at_z(-1))

    def finish():
        total = weighted(0)
        for n, k in ((5, 1), (6, 7), (4, 2), (3, 6), (2, 3)):
            sums[0, k].wait_recv()
            total = total + came[n].astype(F32)
        mixed[...] = total.astype(BF16)

    stages = {
        "a": x_start, "b": x_forward, "c": x_last, "m": first_half, "e": hidden_forward, "f": second_half,
    }
    for word in SCHEDULE:
        kind, number = word[0], int(word[1:])
        if kind == "z":
            hop(number)
        elif kind == "p":
            pick(number // 4, number % 4)
        elif kind == "s":
            (near_sums, far_sums, finish)[number]()
        else:
            stages[kind](number // 4, number % 4)
    for copy in sent:
        copy.wait_send()


COPIES = 176


def shards(tokens, gate_weight, up_weight, down_weight, routes, route_weights, slot_counts):
    row_count, width = tokens.shape
    _, depth, units = gate_weight.shape
    hidden = down_weight.shape[1]
    vmem = pl.BlockSpec(memory_space=pltpu.VMEM)
    hbm = pl.BlockSpec(memory_space=pl.ANY)
    span = PER * row_count
    return pl.pallas_call(
        kernel,
        out_shape=jax.ShapeDtypeStruct((row_count, width), BF16),
        in_specs=[vmem] * 4 + [hbm] * 3,
        out_specs=vmem,
        scratch_shapes=[
            pltpu.VMEM((NZ * row_count, width + TAG), BF16),
            pltpu.VMEM((depth, units), BF16),
            pltpu.VMEM((depth, units), BF16),
            pltpu.VMEM((hidden, width), BF16),
            pltpu.VMEM((TAG, span), F32),
            pltpu.VMEM((G, NY, Q, span), BF16),
            pltpu.VMEM((G, NY, span, Q), BF16),
            pltpu.VMEM((G, NY - 1, Q, width), BF16),
            pltpu.VMEM((G, NX, 2, NY * Q, width), BF16),
            pltpu.VMEM((G, NX, 2, NY * Q, units), BF16),
            pltpu.VMEM((G, NY - 1, Q, width), BF16),
            pltpu.VMEM((G, NY, Q, width), BF16),
            pltpu.VMEM((NZ, row_count, width), BF16),
            pltpu.VMEM((NZ - 1, row_count, width), BF16),
            pltpu.SemaphoreType.DMA((3,)),
            pltpu.SemaphoreType.DMA((COPIES,)),
            pltpu.SemaphoreType.DMA((COPIES,)),
        ],
        compiler_params=pltpu.CompilerParams(
            collective_id=0, has_side_effects=True, vmem_limit_bytes=60 * 1024 * 1024
        ),
    )(tokens, routes.T, route_weights.T, slot_counts[None, :], gate_weight, up_weight, down_weight)


def solution(mesh):
    placed = (
        P("ep", "dp"),
        P("ep", None, "dp"),
        P("ep", None, "dp"),
        P("ep", None, "dp"),
        P("ep", None),
        P("ep", None),
        P("ep"),
    )
    return jax.shard_map(
        shards, mesh=mesh, in_specs=placed, out_specs=P("ep", "dp"), check_vma=False
    )
```

time: 417 us -> 112 us (0.27)
  the two profiles are of different devices: /device:TPU:40 before, /device:TPU:1 now
where the time goes in v2:
time: 112 us
  Pallas kernels  111 us (99%)
  local copies, waits for them, and re-layouts  1.55 us (1%)
    pallas_call x1, Pallas kernels, shards(): pl.pallas_call(kernel, out_shape=jax.ShapeDtypeStruct((row_count, width),...  111 us

profile of v2, /device:TPU:1, one launch (start us, length us, event | category | flops | bytes accessed | tf_op | source)
XLA Modules:
  0.0 112.3 jit_solution(12769856290630835907)
XLA Ops:
  0.0 110.8 %shard_map.73 = bf16[64,896]{1,0:T(8,128)(2,1)} custom-call(bf16[64,896]{1,0:T(8,128)(2,1)} %tokens.1, s32[8,64]{1,0:T(8,128)} %bitcast.3, f32[8,64]{1,0:T(8,128)} %bitcast.4, s32[1,64]{1,0:T(1,128)} %bitcast.5, bf16[1,7168,256]{2,1,0:T(8,128)(2,1)} %gate.1, bf16[1,7168,256]{2,1,0:T(8,128)(2,1)} %up.1, bf16[1,2048,896]{2,1,0:T(8,128)(2,1)} %down.1), custom_call_target="tpu_custom_call" | custom-call | tf_op jit(solution)/shard_map/pallas_call | solution.py:324
  110.8 1.6 %copy.9 = bf16[64,896]{1,0:T(8,128)(2,1)} copy(bf16[64,896]{1,0:T(8,128)(2,1)} %shard_map.73) | data formatting | bytes 229376

commit v3 on v2

--- a/solution.py
+++ b/solution.py
@@ -10,6 +10,7 @@
 CAP = 20
 EXPERTS = 32
 TAG = 128
+EARLY = 256
 GROUPS = ((0, 1, 7, 2), (6, 3, 5, 4))
 BLOCKS = GROUPS[0] + GROUPS[1]
 G = len(GROUPS)
@@ -17,26 +18,30 @@
 Q = PER * CAP
 SIDE = (0, 1, 3, 2)
 MARK = 1024.0
-DIRECT = ((0, 3), (0, 2))
+DIRECT = ((1, 2), (1, 3),)
+RING_DIRECT = ()
 F32 = jnp.float32
 BF16 = jnp.bfloat16
 SCHEDULE = (
-    "z1", "z2", "p0", "a0", "p1", "p3", "p2", "z3", "b0", "a1", "z4", "p4", "a4", "p5", "p7", "p6", "c0",
-    "b1", "a5", "m0", "c1", "b4", "a6", "e0", "m1", "c4", "b5", "a7", "f0", "e1", "m4", "c5", "b6", "a3",
-    "f1", "e4", "m5", "c6", "b7", "a2", "f4", "e5", "m6", "c7", "b3", "f5", "e6", "m7", "c3", "b2", "f6",
-    "e7", "m3", "f7", "c2", "e3", "m2", "f3", "s1", "e2", "f2", "s0", "s2",
+    "g0", "z1", "g1", "z2", "p0", "p3", "p2", "p1", "a0", "g2", "q0", "q2", "q1", "q3", "h0", "a1", "z3",
+    "b0", "a2", "a3", "g3", "z4", "p4", "p7", "p5", "p6", "b1", "h3", "c0", "g4", "q4", "q7", "q6", "q5",
+    "a4", "h4", "m0", "b2", "h2", "h1", "b3", "c1", "a5", "m1", "b4", "e0", "a6", "c2", "c3", "h5", "m2",
+    "b5", "m3", "e1", "h7", "h6", "c4", "a7", "d0", "m4", "f0", "b6", "c5", "e2", "m5", "d1", "e3", "f1",
+    "b7", "e4", "d3", "c6", "f3", "d2", "e5", "m6", "d4", "c7", "f2", "f4", "d5", "m7", "e6", "f5", "d6",
+    "f6", "e7", "s0", "d7", "f7", "s1", "s3", "s2",
 )
 
 
 def kernel(
     tokens, routes, weights, counts, gate, up, down, mixed,
-    rows, gate_w, up_w, down_w, place_t, choose, choose_t, picked, gath, hid, outs, back, part, came,
+    rows, early, gate_w, up_w, down_w, place_t, choose, choose_t, picked, picked_e, gath, gath_e, hid, outs, back, part, came,
     load_sem, send, recv,
 ):
     row_count, width = tokens.shape
     units = gate_w.shape[1]
     top = routes.shape[0]
     span = PER * row_count
+    main = width - EARLY
     ep, dp = lax.axis_index("ep"), lax.axis_index("dp")
     z, y, x, core = ep // NY, ep % NY, dp // 2, dp % 2
     used = [0]
@@ -88,39 +93,58 @@
     low = dense - high - middle
     term = lax.broadcasted_iota(jnp.int32, (row_count, TAG), 1) // EXPERTS
     tag = jnp.where(term == 0, high, jnp.where(term == 1, middle, jnp.where(term == 2, low, 0.0)))
-    rows[pl.ds(0, row_count), pl.ds(width, TAG)] = tag.astype(BF16)
-    rows[pl.ds(0, row_count), pl.ds(0, width)] = tokens[...]
+    rows[pl.ds(0, row_count), pl.ds(main, TAG)] = tag.astype(BF16)
+    rows[pl.ds(0, row_count), pl.ds(0, main)] = tokens[:, :main]
+    early[pl.ds(0, row_count), pl.ds(0, EARLY)] = tokens[:, main:]
 
     pl.semaphore_wait(barrier, len(partners))
 
     half_rows = row_count // 2
 
-    def block(k, h):
-        return rows.at[pl.ds(BLOCKS.index(k) * row_count + h * half_rows, half_rows)]
+    def block(ref, k, h):
+        return ref.at[pl.ds(BLOCKS.index(k) * row_count + h * half_rows, half_rows)]
 
     moves = {}
 
-    def onward(k, h, step):
-        moves[(k + step) % NZ, h] = go(block(k, h), block((k + step) % NZ, h), at_z(-step))
-
-    for h in (0, 1):
-        onward(0, h, 1)
-        onward(0, 1 - h, -1)
-
-    def hop(k):
+    def onward(ref, name, k, h, step):
+        to = (k + step) % NZ
+        moves[name, to, h] = go(block(ref, k, h), block(ref, to, h), at_z(-step))
+
+    def first_hop(ref, name):
         for h in (0, 1):
+            onward(ref, name, 0, h, 1)
+            onward(ref, name, 0, 1 - h, -1)
+
+    def hop(ref, name, k):
+        for h in (0, 1):
+            moves[name, k, h].wait_recv()
             if k < NZ // 2:
-                moves[k, h].wait_recv()
                 if k < NZ // 2 - 1 or h == 0:
-                    onward(k, h, 1)
-                moves[NZ - k, 1 - h].wait_recv()
+                    onward(ref, name, k, h, 1)
+                moves[name, NZ - k, 1 - h].wait_recv()
                 if k < NZ // 2 - 1 or h == 0:
-                    onward(NZ - k, 1 - h, -1)
-            else:
-                moves[k, h].wait_recv()
+                    onward(ref, name, NZ - k, 1 - h, -1)
+
+    first_hop(rows, "main")
+
+    own_rows = pl.ds(0, row_count)
+
+    def early_at(dx):
+        return pl.ds(dx * EARLY, EARLY)
+
+    own_early = early.at[own_rows, early_at(0)]
+    gathered = [go(own_early, early.at[own_rows, early_at(NX - step)], at_x(step)) for step in (1, 3, 2)]
+
+    def early_hop(k):
+        if k == 0:
+            for copy in gathered:
+                copy.wait_recv()
+            first_hop(early, "early")
+        else:
+            hop(early, "early", k)
 
     def group_tags(g):
-        return rows[pl.ds(g * span, span), pl.ds(width, TAG)]
+        return rows[pl.ds(g * span, span), pl.ds(main, TAG)]
 
     def places(g):
         taken = jnp.where(group_tags(g).astype(F32) > 0.0, 1.0, 0.0).astype(BF16)
@@ -147,7 +171,7 @@
     def pick(g, j):
         if j == 0:
             places(g)
-        source = rows[pl.ds(g * span, span), pl.ds(0, width)]
+        source = rows[pl.ds(g * span, span), pl.ds(0, main)]
         chosen = jnp.dot(choose[g, j], source, preferred_element_type=F32).astype(BF16)
         q = SIDE.index((NY - j) % NY)
         if j == 0:
@@ -156,6 +180,23 @@
             picked[g, j - 1] = chosen
             to_expert[g, q] = go(picked.at[g, j - 1], gath.at[g, 0, 0, spot(q)], at_y(j))
 
+    early_to = {}
+    early_shared = {}
+
+    def pick_early(g, j):
+        chosen = jnp.dot(choose[g, j], early[pl.ds(g * span, span), :], preferred_element_type=F32).astype(BF16)
+        q = SIDE.index((NY - j) % NY)
+        if j == 0:
+            gath_e[g, 0, spot(q), :] = chosen
+        else:
+            picked_e[g, j - 1] = chosen
+            early_to[g, q] = go(picked_e.at[g, j - 1], gath_e.at[g, 0, spot(q)], at_y(j))
+
+    def early_share(g, q):
+        if (g, q) in early_to:
+            early_to[g, q].wait_recv()
+        early_shared[g, q] = go(gath_e.at[g, 0, spot(q)], gath_e.at[g, 1, spot(q)], other)
+
     ring = {}
 
     def x_start(g, q):
@@ -165,6 +206,8 @@
         mine = gath.at[g, 0, 0, at]
         ring[g, q, 3, 0] = go(mine, gath.at[g, 3, 0, at], at_x(1))
         ring[g, q, 1, 0] = go(mine, gath.at[g, 1, 0, at], at_x(-1))
+        if (g, q) in RING_DIRECT:
+            ring[g, q, 2, 0] = go(mine, gath.at[g, 2, 0, at], at_x(2))
         ring[g, q, 0, 1] = go(mine, gath.at[g, 0, 1, at], other)
 
     def share(g, q, dx):
@@ -174,11 +217,11 @@
     def x_forward(g, q):
         at = spot(q)
         ring[g, q, 3, 0].wait_recv()
-        if q % 2 == 0:
+        if (g, q) not in RING_DIRECT and q % 2 == 0:
             ring[g, q, 2, 0] = go(gath.at[g, 3, 0, at], gath.at[g, 2, 0, at], at_x(1))
         share(g, q, 3)
         ring[g, q, 1, 0].wait_recv()
-        if q % 2 == 1:
+        if (g, q) not in RING_DIRECT and q % 2 == 1:
             ring[g, q, 2, 0] = go(gath.at[g, 1, 0, at], gath.at[g, 2, 0, at], at_x(-1))
         share(g, q, 1)
 
@@ -200,12 +243,18 @@
             for load in loads:
                 load.wait()
         at = spot(q)
+        early_shared[g, q].wait_recv()
         gate_acc = jnp.zeros((Q, units), F32)
         up_acc = jnp.zeros((Q, units), F32)
         for dx, dc in STEPS:
+            deep = pl.ds(pl.multiple_of(slice_at(dx, dc) * width + main, EARLY // 2), EARLY)
+            piece = gath_e[g, dc, at, early_at(dx)]
+            gate_acc = gate_acc + jnp.dot(piece, gate_w[deep, :], preferred_element_type=F32)
+            up_acc = up_acc + jnp.dot(piece, up_w[deep, :], preferred_element_type=F32)
+        for dx, dc in STEPS:
             if dc == 1:
                 ring[g, q, dx, 1].wait_recv()
-            deep = pl.ds(pl.multiple_of(slice_at(dx, dc) * width, width), width)
+            deep = pl.ds(pl.multiple_of(slice_at(dx, dc) * width, width), main)
             piece = gath[g, dx, dc, at, :]
             gate_acc = gate_acc + jnp.dot(piece, gate_w[deep, :], preferred_element_type=F32)
             up_acc = up_acc + jnp.dot(piece, up_w[deep, :], preferred_element_type=F32)
@@ -225,12 +274,15 @@
                 hops[g, q, 2, 0] = go(hid.at[g, dx, 0, at], hid.at[g, 2, 0, at], at_x(step))
             hops[g, q, dx, 1] = go(hid.at[g, dx, 0, at], hid.at[g, dx, 1, at], other)
 
-    from_expert = {}
-
-    def second_half(g, q):
+    def hidden_last(g, q):
         at = spot(q)
         hops[g, q, 2, 0].wait_recv()
         hops[g, q, 2, 1] = go(hid.at[g, 2, 0, at], hid.at[g, 2, 1, at], other)
+
+    from_expert = {}
+
+    def second_half(g, q):
+        at = spot(q)
         acc = jnp.zeros((Q, width), F32)
         for dx, dc in STEPS:
             if dc == 1:
@@ -247,7 +299,7 @@
     def weighted(k):
         n = BLOCKS.index(k)
         g, at = n // PER, pl.ds(n % PER * row_count, row_count)
-        tags = rows[pl.ds(n * row_count, row_count), pl.ds(width, TAG)].astype(F32)
+        tags = rows[pl.ds(n * row_count, row_count), pl.ds(main, TAG)].astype(F32)
         lanes = lax.broadcasted_iota(jnp.int32, (row_count, TAG), 1) % EXPERTS
         total = jnp.zeros((row_count, width), F32)
         for j in range(NY):
@@ -269,6 +321,8 @@
         sums[3] = go(part.at[4], came.at[0], at_z(1))
         part[5] = weighted(5).astype(BF16)
         sums[6] = go(part.at[5], came.at[1], at_z(-1))
+
+    def far_ends():
         mine = weighted(3)
         sums[3].wait_recv()
         part[3] = (mine + came[0].astype(F32)).astype(BF16)
@@ -295,23 +349,26 @@
         mixed[...] = total.astype(BF16)
 
     stages = {
-        "a": x_start, "b": x_forward, "c": x_last, "m": first_half, "e": hidden_forward, "f": second_half,
+        "q": pick_early, "h": early_share, "a": x_start, "b": x_forward, "c": x_last, "m": first_half, "e": hidden_forward,
+        "d": hidden_last, "f": second_half,
     }
     for word in SCHEDULE:
         kind, number = word[0], int(word[1:])
         if kind == "z":
-            hop(number)
+            hop(rows, "main", number)
+        elif kind == "g":
+            early_hop(number)
         elif kind == "p":
             pick(number // 4, number % 4)
         elif kind == "s":
-            (near_sums, far_sums, finish)[number]()
+            (near_sums, far_sums, finish, far_ends)[number]()
         else:
             stages[kind](number // 4, number % 4)
     for copy in sent:
         copy.wait_send()
 
 
-COPIES = 176
+COPIES = 220
 
 
 def shards(tokens, gate_weight, up_weight, down_weight, routes, route_weights, slot_counts):
@@ -321,21 +378,25 @@
     vmem = pl.BlockSpec(memory_space=pltpu.VMEM)
     hbm = pl.BlockSpec(memory_space=pl.ANY)
     span = PER * row_count
+    main = width - EARLY
     return pl.pallas_call(
         kernel,
         out_shape=jax.ShapeDtypeStruct((row_count, width), BF16),
         in_specs=[vmem] * 4 + [hbm] * 3,
         out_specs=vmem,
         scratch_shapes=[
-            pltpu.VMEM((NZ * row_count, width + TAG), BF16),
+            pltpu.VMEM((NZ * row_count, main + TAG), BF16),
+            pltpu.VMEM((NZ * row_count, NX * EARLY), BF16),
             pltpu.VMEM((depth, units), BF16),
             pltpu.VMEM((depth, units), BF16),
             pltpu.VMEM((hidden, width), BF16),
             pltpu.VMEM((TAG, span), F32),
             pltpu.VMEM((G, NY, Q, span), BF16),
             pltpu.VMEM((G, NY, span, Q), BF16),
-            pltpu.VMEM((G, NY - 1, Q, width), BF16),
-            pltpu.VMEM((G, NX, 2, NY * Q, width), BF16),
+            pltpu.VMEM((G, NY - 1, Q, main), BF16),
+            pltpu.VMEM((G, NY - 1, Q, NX * EARLY), BF16),
+            pltpu.VMEM((G, NX, 2, NY * Q, main), BF16),
+            pltpu.VMEM((G, 2, NY * Q, NX * EARLY), BF16),
             pltpu.VMEM((G, NX, 2, NY * Q, units), BF16),
             pltpu.VMEM((G, NY - 1, Q, width), BF16),
             pltpu.VMEM((G, NY, Q, width), BF16),

time: 112 us -> 96.8 us (0.86)
  the two profiles are of different devices: /device:TPU:1 before, /device:TPU:40 now
where the time goes in v3:
time: 96.8 us; the launch traced here: 95 us
  Pallas kernels  93.4 us (96%)
  local copies, waits for them, and re-layouts  1.55 us (2%)
    pallas_call x1, Pallas kernels, shards(): pl.pallas_call(kernel, out_shape=jax.ShapeDtypeStruct((row_count, width),...  93.4 us

profile of v3, /device:TPU:40, one launch (start us, length us, event | category | flops | bytes accessed | tf_op | source)
XLA Modules:
  0.0 95.0 jit_solution(7926943259516882807)
XLA Ops:
  0.0 93.4 %shard_map.73 = bf16[64,896]{1,0:T(8,128)(2,1)} custom-call(bf16[64,896]{1,0:T(8,128)(2,1)} %tokens.1, s32[8,64]{1,0:T(8,128)} %bitcast.3, f32[8,64]{1,0:T(8,128)} %bitcast.4, s32[1,64]{1,0:T(1,128)} %bitcast.5, bf16[1,7168,256]{2,1,0:T(8,128)(2,1)} %gate.1, bf16[1,7168,256]{2,1,0:T(8,128)(2,1)} %up.1, bf16[1,2048,896]{2,1,0:T(8,128)(2,1)} %down.1), custom_call_target="tpu_custom_call" | custom-call | tf_op jit(solution)/shard_map/pallas_call | solution.py:382
  93.5 1.6 %copy.9 = bf16[64,896]{1,0:T(8,128)(2,1)} copy(bf16[64,896]{1,0:T(8,128)(2,1)} %shard_map.73) | data formatting | bytes 229376

commit v4 on v3

--- a/solution.py
+++ b/solution.py
@@ -18,6 +18,7 @@
 Q = PER * CAP
 SIDE = (0, 1, 3, 2)
 MARK = 1024.0
+COLUMNS = ((0, 512), (512, 384))
 DIRECT = ((1, 2), (1, 3),)
 RING_DIRECT = ()
 F32 = jnp.float32
@@ -28,7 +29,7 @@
     "a4", "h4", "m0", "b2", "h2", "h1", "b3", "c1", "a5", "m1", "b4", "e0", "a6", "c2", "c3", "h5", "m2",
     "b5", "m3", "e1", "h7", "h6", "c4", "a7", "d0", "m4", "f0", "b6", "c5", "e2", "m5", "d1", "e3", "f1",
     "b7", "e4", "d3", "c6", "f3", "d2", "e5", "m6", "d4", "c7", "f2", "f4", "d5", "m7", "e6", "f5", "d6",
-    "f6", "e7", "s0", "d7", "f7", "s1", "s3", "s2",
+    "f6", "e7", "s0", "d7", "f7", "s1", "s4", "s3", "s5", "s2",
 )
 
 
@@ -247,7 +248,7 @@
         gate_acc = jnp.zeros((Q, units), F32)
         up_acc = jnp.zeros((Q, units), F32)
         for dx, dc in STEPS:
-            deep = pl.ds(pl.multiple_of(slice_at(dx, dc) * width + main, EARLY // 2), EARLY)
+            deep = pl.ds(pl.multiple_of(slice_at(dx, dc) * width + main, 128), EARLY)
             piece = gath_e[g, dc, at, early_at(dx)]
             gate_acc = gate_acc + jnp.dot(piece, gate_w[deep, :], preferred_element_type=F32)
             up_acc = up_acc + jnp.dot(piece, up_w[deep, :], preferred_element_type=F32)
@@ -294,63 +295,83 @@
             back[g, 0] = acc.astype(BF16)
         else:
             outs[g, r - 1] = acc.astype(BF16)
-            from_expert[g, NY - r] = go(outs.at[g, r - 1], back.at[g, NY - r], at_y(r))
-
-    def weighted(k):
-        n = BLOCKS.index(k)
-        g, at = n // PER, pl.ds(n % PER * row_count, row_count)
-        tags = rows[pl.ds(n * row_count, row_count), pl.ds(main, TAG)].astype(F32)
+            for n, columns in enumerate(COLUMNS):
+                cut = pl.ds(0, Q), pl.ds(*columns)
+                from_expert[g, NY - r, n] = go(
+                    outs.at[(g, r - 1) + cut], back.at[(g, NY - r) + cut], at_y(r)
+                )
+
+    def weighted(k, start, size):
+        order = BLOCKS.index(k)
+        g, at = order // PER, pl.ds(order % PER * row_count, row_count)
+        tags = rows[pl.ds(order * row_count, row_count), pl.ds(main, TAG)].astype(F32)
         lanes = lax.broadcasted_iota(jnp.int32, (row_count, TAG), 1) % EXPERTS
-        total = jnp.zeros((row_count, width), F32)
+        total = jnp.zeros((row_count, size), F32)
         for j in range(NY):
             expert = z * NY + (y + j) % NY
             scale = jnp.sum(jnp.where(lanes == expert, tags, 0.0), axis=1, keepdims=True)
-            fetched = jnp.dot(choose_t[g, j, at, :], back[g, j], preferred_element_type=F32)
+            fetched = jnp.dot(choose_t[g, j, at, :], back[g, j, :, pl.ds(start, size)], preferred_element_type=F32)
             total = total + scale * fetched
         return total
 
-    def returned(g):
+    def returned(g, n):
         for j in range(1, NY):
-            from_expert[g, j].wait_recv()
+            from_expert[g, j, n].wait_recv()
+
+    def piece_of(ref, place, n):
+        return ref.at[place, pl.ds(0, row_count), pl.ds(*COLUMNS[n])]
 
     sums = {}
 
-    def far_sums():
-        returned(1)
-        part[4] = weighted(4).astype(BF16)
-        sums[3] = go(part.at[4], came.at[0], at_z(1))
-        part[5] = weighted(5).astype(BF16)
-        sums[6] = go(part.at[5], came.at[1], at_z(-1))
-
-    def far_ends():
-        mine = weighted(3)
-        sums[3].wait_recv()
-        part[3] = (mine + came[0].astype(F32)).astype(BF16)
-        sums[0, 3] = go(part.at[3], came.at[2], at_z(3))
-        mine = weighted(6)
-        sums[6].wait_recv()
-        part[6] = (mine + came[1].astype(F32)).astype(BF16)
-        sums[0, 6] = go(part.at[6], came.at[3], at_z(-2))
+    def far_sums(n):
+        returned(1, n)
+        cut = pl.ds(*COLUMNS[n])
+        part[4, :, cut] = weighted(4, *COLUMNS[n]).astype(BF16)
+        sums[3, n] = go(piece_of(part, 4, n), piece_of(came, 0, n), at_z(1))
+        part[5, :, cut] = weighted(5, *COLUMNS[n]).astype(BF16)
+        sums[6, n] = go(piece_of(part, 5, n), piece_of(came, 1, n), at_z(-1))
+
+    def far_ends(n):
+        cut = pl.ds(*COLUMNS[n])
+        mine = weighted(3, *COLUMNS[n])
+        sums[3, n].wait_recv()
+        part[3, :, cut] = (mine + came[0, :, cut].astype(F32)).astype(BF16)
+        sums[0, 3, n] = go(piece_of(part, 3, n), piece_of(came, 2, n), at_z(3))
+        mine = weighted(6, *COLUMNS[n])
+        sums[6, n].wait_recv()
+        part[6, :, cut] = (mine + came[1, :, cut].astype(F32)).astype(BF16)
+        sums[0, 6, n] = go(piece_of(part, 6, n), piece_of(came, 3, n), at_z(-2))
 
     def near_sums():
-        returned(0)
-        part[2] = weighted(2).astype(BF16)
+        returned(0, 0)
+        returned(0, 1)
+        part[2] = weighted(2, 0, width).astype(BF16)
         sums[0, 2] = go(part.at[2], came.at[4], at_z(2))
-        part[1] = weighted(1).astype(BF16)
+        part[1] = weighted(1, 0, width).astype(BF16)
         sums[0, 1] = go(part.at[1], came.at[5], at_z(1))
-        part[7] = weighted(7).astype(BF16)
+        part[7] = weighted(7, 0, width).astype(BF16)
         sums[0, 7] = go(part.at[7], came.at[6], at_z(-1))
 
     def finish():
-        total = weighted(0)
-        for n, k in ((5, 1), (6, 7), (4, 2), (3, 6), (2, 3)):
+        for k in (1, 7, 2):
             sums[0, k].wait_recv()
-            total = total + came[n].astype(F32)
-        mixed[...] = total.astype(BF16)
-
+        for n, columns in enumerate(COLUMNS):
+            cut = pl.ds(*columns)
+            total = weighted(0, *columns)
+            for place in (5, 6, 4):
+                total = total + came[place, :, cut].astype(F32)
+            sums[0, 6, n].wait_recv()
+            total = total + came[3, :, cut].astype(F32)
+            sums[0, 3, n].wait_recv()
+            mixed[:, cut] = (total + came[2, :, cut].astype(F32)).astype(BF16)
+
+    endings = {
+        "s0": near_sums, "s1": lambda: far_sums(0), "s4": lambda: far_sums(1),
+        "s3": lambda: far_ends(0), "s5": lambda: far_ends(1), "s2": finish,
+    }
     stages = {
-        "q": pick_early, "h": early_share, "a": x_start, "b": x_forward, "c": x_last, "m": first_half, "e": hidden_forward,
-        "d": hidden_last, "f": second_half,
+        "q": pick_early, "h": early_share, "a": x_start, "b": x_forward, "c": x_last, "m": first_half,
+        "e": hidden_forward, "d": hidden_last, "f": second_half,
     }
     for word in SCHEDULE:
         kind, number = word[0], int(word[1:])
@@ -361,7 +382,7 @@
         elif kind == "p":
             pick(number // 4, number % 4)
         elif kind == "s":
-            (near_sums, far_sums, finish, far_ends)[number]()
+            endings[word]()
         else:
             stages[kind](number // 4, number % 4)
     for copy in sent:

time: 96.8 us -> 95.1 us (0.982)
  Pallas kernels: 93.4 us -> 92.3 us
    pallas_call x1, Pallas kernels: 93.4 us -> 92.3 us  [shards(): pl.pallas_call(kernel, out_shape=jax.ShapeDtypeStruct((row_count, width),...]
where the time goes in v4:
time: 95.1 us; the launch traced here: 93.9 us
  Pallas kernels  92.3 us (97%)
  local copies, waits for them, and re-layouts  1.55 us (2%)
    pallas_call x1, Pallas kernels, shards(): pl.pallas_call(kernel, out_shape=jax.ShapeDtypeStruct((row_count, width),...  92.3 us

profile of v4, /device:TPU:40, one launch (start us, length us, event | category | flops | bytes accessed | tf_op | source)
XLA Modules:
  0.0 93.9 jit_solution(13725511050246841815)
XLA Ops:
  0.0 92.3 %shard_map.73 = bf16[64,896]{1,0:T(8,128)(2,1)} custom-call(bf16[64,896]{1,0:T(8,128)(2,1)} %tokens.1, s32[8,64]{1,0:T(8,128)} %bitcast.3, f32[8,64]{1,0:T(8,128)} %bitcast.4, s32[1,64]{1,0:T(1,128)} %bitcast.5, bf16[1,7168,256]{2,1,0:T(8,128)(2,1)} %gate.1, bf16[1,7168,256]{2,1,0:T(8,128)(2,1)} %up.1, bf16[1,2048,896]{2,1,0:T(8,128)(2,1)} %down.1), custom_call_target="tpu_custom_call" | custom-call | tf_op jit(solution)/shard_map/pallas_call | solution.py:403
  92.3 1.6 %copy.9 = bf16[64,896]{1,0:T(8,128)(2,1)} copy(bf16[64,896]{1,0:T(8,128)(2,1)} %shard_map.73) | data formatting | bytes 229376

commit v5 on v4

--- a/solution.py
+++ b/solution.py
@@ -24,7 +24,7 @@
 F32 = jnp.float32
 BF16 = jnp.bfloat16
 SCHEDULE = (
-    "g0", "z1", "g1", "z2", "p0", "p3", "p2", "p1", "a0", "g2", "q0", "q2", "q1", "q3", "h0", "a1", "z3",
+    "g0", "z1", "g1", "z2", "p0", "a0", "p3", "p1", "p2", "g2", "q0", "q2", "q1", "q3", "h0", "a1", "z3",
     "b0", "a2", "a3", "g3", "z4", "p4", "p7", "p5", "p6", "b1", "h3", "c0", "g4", "q4", "q7", "q6", "q5",
     "a4", "h4", "m0", "b2", "h2", "h1", "b3", "c1", "a5", "m1", "b4", "e0", "a6", "c2", "c3", "h5", "m2",
     "b5", "m3", "e1", "h7", "h6", "c4", "a7", "d0", "m4", "f0", "b6", "c5", "e2", "m5", "d1", "e3", "f1",

time: 95.1 us -> 95.3 us (level)
  no operation moved by 1% of the time
where the time goes in v5:
time: 95.3 us; the launch traced here: 94 us
  Pallas kernels  92.4 us (97%)
  local copies, waits for them, and re-layouts  1.55 us (2%)
    pallas_call x1, Pallas kernels, shards(): pl.pallas_call(kernel, out_shape=jax.ShapeDtypeStruct((row_count, width),...  92.4 us

profile of v5, /device:TPU:40, one launch (start us, length us, event | category | flops | bytes accessed | tf_op | source)
XLA Modules:
  0.0 94.0 jit_solution(8065987898262757320)
XLA Ops:
  0.0 92.4 %shard_map.73 = bf16[64,896]{1,0:T(8,128)(2,1)} custom-call(bf16[64,896]{1,0:T(8,128)(2,1)} %tokens.1, s32[8,64]{1,0:T(8,128)} %bitcast.3, f32[8,64]{1,0:T(8,128)} %bitcast.4, s32[1,64]{1,0:T(1,128)} %bitcast.5, bf16[1,7168,256]{2,1,0:T(8,128)(2,1)} %gate.1, bf16[1,7168,256]{2,1,0:T(8,128)(2,1)} %up.1, bf16[1,2048,896]{2,1,0:T(8,128)(2,1)} %down.1), custom_call_target="tpu_custom_call" | custom-call | tf_op jit(solution)/shard_map/pallas_call | solution.py:403
  92.4 1.6 %copy.9 = bf16[64,896]{1,0:T(8,128)(2,1)} copy(bf16[64,896]{1,0:T(8,128)(2,1)} %shard_map.73) | data formatting | bytes 229376
